TPU v7x, 32 devices: a whole 2x2x4 slice. The times are simulated.
32 devices in a mesh: contacts: 8 (over z, y), tm: 4 (over x, core).
Axes of the slice: x: 2, y: 2, z: 4, core: 2. Of those that a mesh axis runs over, the one named last changes fastest.
Arguments:
- signal: bfloat16 [2048, 512], P('contacts', 'tm'), may hold values from -6 to 6
- pos_idx: int32 [2048], P('contacts'), may hold values from 0 to 4095
- live_count: int32 [8], P('contacts'), may hold values from 128 to 256, as said below
- latents: bfloat16 [256, 512], replicated, may hold values from -400 to 400
- pos_table: bfloat16 [4096, 512], replicated, may hold values from -6 to 6
- w_in: bfloat16 [32, 512], replicated, may hold values from -1 to 1
- w_kv: bfloat16 [512, 1024], replicated, may hold values from -0.25 to 0.25
- w_query: bfloat16 [512, 512], replicated, may hold values from -0.25 to 0.25
- w_out: bfloat16 [512, 512], replicated, may hold values from -0.25 to 0.25
- conv_weight: bfloat16 [2, 3, 512, 512], replicated, may hold values from -0.15625 to 0.15625
- conv_bias: float32 [2, 512], replicated, may hold values from -3 to 3
- cotangent: bfloat16 [16, 256, 512], P('tm', 'contacts'), may hold values from -6 to 6
Outputs:
- features: bfloat16 [16, 256, 512], P('tm', 'contacts')
- d_latents: float32 [256, 512], replicated
Inputs may be any that keep to these rules, and one draw needn't show every extreme that they name: The first live_count[b] contacts of block b are valid; some block is full and some block has exactly 128 valid contacts.
All inputs are finite; a program needn't handle non-finite values.
Results may differ from a plain program's by a relative error of at most 0.018.
The roundings to bfloat16 on the way count: a program that leaves them out, or rounds other values in their place, can miss the bound.
Values may be sent and summed in bfloat16 or wider, within the bound.
A program may use at most 192 MiB of HBM per device.

v0:
```python
import jax
import jax.numpy as jnp
from jax import lax
from jax.sharding import PartitionSpec as P

HD = 64
PATCH = 32
KSIZE = 3
LAYERS = 2


neg_big = -1e30
scale_dot = 0.125


def with_halo(x, sides, width):
    for axis, dim in sides:
        peers, length = (lax.axis_size(axis), x.shape[dim])
        up = [(i, (i + 1) % peers) for i in range(peers - 1)]
        down = [(j, i) for i, j in up]
        last = lax.slice_in_dim(x, length - width, length, axis=dim)
        first = lax.slice_in_dim(x, 0, width, axis=dim)
        before = lax.ppermute(last, axis, up)
        after = lax.ppermute(first, axis, down)
        x = jnp.concatenate([before, x, after], axis=dim)
    return x


def silu_slope(pre_act):
    sigmoid_v = jax.nn.sigmoid(pre_act)
    return sigmoid_v * (1.0 + pre_act * (1.0 - sigmoid_v))


def split_heads(values, head_count):
    return values.reshape(values.shape[:-1] + (head_count, values.shape[-1] // head_count))


def normalize(accum_out, totals):
    head_count = totals.shape[-1]
    return (
        (split_heads(accum_out, head_count) / totals[..., None])
        .reshape(accum_out.shape)
        .astype(jnp.bfloat16)
    )


def conv_apply(source, weight, bias_row, dilation, out_count):
    stacked = jnp.stack(
        [source[j * dilation : j * dilation + out_count] for j in range(KSIZE)], axis=2
    )
    return (
        jnp.einsum("tlji,jio->tlo", stacked, weight, preferred_element_type=jnp.float32) + bias_row
    )


def local(
    signal,
    pos_idx,
    live_count,
    latents,
    pos_table,
    w_in,
    w_kv,
    w_query,
    w_out,
    conv_weight,
    conv_bias,
    cotangent,
):
    con_dev = signal.shape[0]
    pat_dev = signal.shape[1] // PATCH
    model_width = w_query.shape[0]
    head_count = model_width // HD
    lat_rows = latents.shape[0]
    groups = lax.axis_size("contacts")
    lat_dev = lat_rows // groups
    is_valid = jnp.arange(con_dev, dtype=jnp.int32) < live_count[0]
    embedded = jnp.einsum(
        "cpt,td->pcd",
        signal.reshape(con_dev, pat_dev, PATCH),
        w_in,
        preferred_element_type=jnp.float32,
    )
    pos_rows = jnp.take(pos_table, pos_idx, axis=0).astype(jnp.float32)
    tokens = (embedded + pos_rows[None]).astype(jnp.bfloat16)
    keyval = jnp.dot(
        tokens.reshape(pat_dev * con_dev, model_width), w_kv, preferred_element_type=jnp.float32
    ).astype(jnp.bfloat16)
    keyval = keyval.reshape(pat_dev // 2, 2, con_dev, 2, head_count, HD)
    queries = (
        jnp.dot(latents, w_query, preferred_element_type=jnp.float32)
        .astype(jnp.bfloat16)
        .reshape(lat_rows, head_count, HD)
    )

    def masked_scores(key_block):
        scores = (
            jnp.einsum("ihe,pche->phic", queries, key_block, preferred_element_type=jnp.float32)
            * scale_dot
        )
        return jnp.where(is_valid, scores, neg_big)

    def attend(kv_block):
        scores = masked_scores(kv_block[:, :, 0])
        top_score = jnp.max(scores, axis=3)
        weights = jnp.where(is_valid, jnp.exp(scores - top_score[..., None]), 0.0)
        totals = jnp.sum(weights, axis=3)
        accum_out = jnp.einsum(
            "phic,pche->pihe",
            weights.astype(jnp.bfloat16),
            kv_block[:, :, 1],
            preferred_element_type=jnp.float32,
        )
        return (
            jnp.swapaxes(top_score, 1, 2),
            jnp.swapaxes(totals, 1, 2),
            accum_out.reshape(2, lat_rows, model_width),
        )

    top_score, totals, accum_out = lax.map(attend, keyval)
    top_score = top_score.reshape(pat_dev, lat_rows, head_count)
    totals = totals.reshape(pat_dev, lat_rows, head_count)
    accum_out = accum_out.reshape(pat_dev, lat_rows, model_width)
    got_top, got_total, got_acc = (
        lax.all_to_all(top_score[None], "contacts", split_axis=2, concat_axis=0, tiled=True),
        lax.all_to_all(totals[None], "contacts", split_axis=2, concat_axis=0, tiled=True),
        lax.all_to_all(accum_out[None], "contacts", split_axis=2, concat_axis=0, tiled=True),
    )
    own_top = jnp.max(got_top, axis=0)
    factor = jnp.exp(got_top - own_top[None])
    own_total = jnp.sum(got_total * factor, axis=0)
    own_acc = jnp.sum(split_heads(got_acc, head_count) * factor[..., None], axis=0).reshape(
        pat_dev, lat_dev, model_width
    )
    attended = normalize(own_acc, own_total)
    start_x = (
        jnp.dot(
            attended.reshape(pat_dev * lat_dev, model_width),
            w_out,
            preferred_element_type=jnp.float32,
        )
        .astype(jnp.bfloat16)
        .reshape(pat_dev, lat_dev, model_width)
    )
    hidden_list = []
    current = start_x
    for layer_no in range(LAYERS):
        dilation = 2**layer_no
        padded = with_halo(current, (("tm", 0),), dilation * (KSIZE // 2))
        pre_act = conv_apply(padded, conv_weight[layer_no], conv_bias[layer_no], dilation, pat_dev)
        current = (current.astype(jnp.float32) + jax.nn.silu(pre_act)).astype(jnp.bfloat16)
        hidden_list.append(pre_act)
    grad_now = cotangent.astype(jnp.float32)
    for layer_no in reversed(range(LAYERS)):
        dilation = 2**layer_no
        grad_pre = (grad_now * silu_slope(hidden_list[layer_no])).astype(jnp.bfloat16)
        padded = with_halo(grad_pre, (("tm", 0),), dilation * (KSIZE // 2))
        stacked = jnp.stack(
            [
                padded[(KSIZE - 1 - j) * dilation : (KSIZE - 1 - j) * dilation + pat_dev]
                for j in range(KSIZE)
            ],
            axis=2,
        )
        grad_now = grad_now + jnp.einsum(
            "tljo,jio->tli", stacked, conv_weight[layer_no], preferred_element_type=jnp.float32
        )
    grad_att = lax.dot_general(
        grad_now.astype(jnp.bfloat16).reshape(pat_dev * lat_dev, model_width),
        w_out,
        (((1,), (1,)), ((), ())),
        preferred_element_type=jnp.float32,
    )
    grad_att = grad_att.astype(jnp.bfloat16).reshape(pat_dev, lat_dev, model_width)
    grad_all, attended_all = (
        lax.all_gather(grad_att, "contacts", axis=1, tiled=True),
        lax.all_gather(attended, "contacts", axis=1, tiled=True),
    )
    top_all, total_all = (
        lax.all_gather(own_top, "contacts", axis=1, tiled=True),
        lax.all_gather(own_total, "contacts", axis=1, tiled=True),
    )
    delta_row = jnp.sum(
        split_heads(grad_all.astype(jnp.float32), head_count)
        * split_heads(attended_all.astype(jnp.float32), head_count),
        axis=3,
    )

    def back_block(dq_sum, parts):
        kv_block, grad_block, top_block, total_block, delta_block = parts
        key_block = kv_block[:, :, 0]
        scores = masked_scores(key_block)
        top_now = jnp.swapaxes(top_block, 1, 2)
        total_now = jnp.swapaxes(total_block, 1, 2)
        prob_vals = jnp.where(
            is_valid, jnp.exp(scores - top_now[..., None]) / total_now[..., None], 0.0
        )
        grad_prob = jnp.einsum(
            "pihe,pche->phic",
            split_heads(grad_block, head_count),
            kv_block[:, :, 1],
            preferred_element_type=jnp.float32,
        )
        delta_now = jnp.swapaxes(delta_block, 1, 2)
        dscore = (prob_vals * (grad_prob - delta_now[..., None])).astype(jnp.bfloat16)
        return (
            dq_sum
            + jnp.einsum("phic,pche->ihe", dscore, key_block, preferred_element_type=jnp.float32),
            None,
        )

    pairs = pat_dev // 2
    dq_sum, unused = lax.scan(
        back_block,
        jnp.zeros((lat_rows, head_count, HD), jnp.float32),
        (
            keyval,
            grad_all.reshape(pairs, 2, lat_rows, model_width),
            top_all.reshape(pairs, 2, lat_rows, head_count),
            total_all.reshape(pairs, 2, lat_rows, head_count),
            delta_row.reshape(pairs, 2, lat_rows, head_count),
        ),
    )
    query_grad = lax.psum((dq_sum * scale_dot).reshape(lat_rows, model_width), ("contacts", "tm"))
    d_latents = lax.dot_general(
        query_grad.astype(jnp.bfloat16),
        w_query,
        (((1,), (1,)), ((), ())),
        preferred_element_type=jnp.float32,
    )
    return (current, d_latents)


def solution(mesh):
    in_specs = (
        P("contacts", "tm"),
        P("contacts"),
        P("contacts"),
        P(),
        P(),
        P(),
        P(),
        P(),
        P(),
        P(),
        P(),
        P("tm", "contacts", None),
    )
    out_specs = (P("tm", "contacts", None), P())
    return jax.shard_map(local, mesh=mesh, in_specs=in_specs, out_specs=out_specs, check_vma=False)
```

profile of v0, /device:TPU:0, one launch (start us, length us, event | category | flops | bytes accessed | tf_op | source)
XLA Modules:
  0.0 310.8 jit_solution(1138860597232935995)
XLA Ops:
  9.6 3.9 %gather_fusion = bf16[256,512]{1,0:T(8,128)(2,1)S(1)} fusion(bf16[4096,512]{1,0:T(8,128)(2,1)} %param.20, s32[1024]{0:T(1024)S(1)} %pad_clamp_fusion), kind=kCustom, calls=%fused_computation | custom fusion | bytes 525312 | tf_op jit(solution)/shard_map/jit(_take)/gather | solution.py:84
  14.2 2.6 convolution_convert_fusion
  16.8 6.4 %reshape.130 = bf16[2,2,256,2,8,64]{5,4,3,2,1,0:T(8,128)(2,1)} reshape(bf16[1024,1024]{1,0:T(8,128)(2,1)} %convolution_convert_fusion) | data formatting | bytes 4194304 | tf_op jit(solution)/shard_map/reshape | solution.py:89
  23.2 4.5 %copy.77 = bf16[2,2,256,2,8,64]{2,5,1,4,3,0:T(8,128)(2,1)S(1)} copy(bf16[2,2,256,2,8,64]{5,4,3,2,1,0:T(8,128)(2,1)} %reshape.130) | data formatting | bytes 4194304
  28.2 12.1 %while.26 = (s32[]{:T(128)}, f32[2,2,256,8]{2,3,1,0:T(8,128)S(1)}, f32[2,2,256,8]{2,1,3,0:T(2,128)S(1)}, f32[2,2,256,512]{2,3,1,0:T(8,128)}, bf16[2,2,256,2,8,64...) while((s32[]{:T(128)}, f32[2,2,256,8]{2,3,1,0:T(8,128)S(1)}, ...), condition=%wide.region_3.4_spmd.clone, body=%wide.region_0.3_spmd.clone.sunk | while | flops 277864704 | bytes 36029600 | solution.py:120
  30.0 1.2 fusion.131
  32.9 1.4 copy-done.7
  36.0 1.2 fusion.131
  38.9 1.4 copy-done.7
  41.7 7.3 %all-to-all-start.1 = ((f32[8,1,1024]{2,1,0:T(1,128)}), f32[8,1,1024]{2,1,0:T(1,128)S(1)}, u32[]{:S(2)}, u32[]{:S(2)}) async-start(f32[8,1,1024]{2,1,0:T(1,128)} %reshape.133), calls=%async_computation.1 | async-start | bytes 65536 | tf_op jit(solution)/shard_map/all_to_all | solution.py:125
  50.5 5.2 %all-to-all-done.1 = f32[8,1,1024]{2,1,0:T(1,128)S(1)} async-done(((f32[8,1,1024]{2,1,0:T(1,128)}), f32[8,1,1024]{2,1,0:T(1,128)S(1)}, u32[]{:S(2)}, u32[]{:S(2)}) %all-to-all-start.1) | async-done | bytes 32800 | tf_op jit(solution)/shard_map/all_to_all | solution.py:125
  55.7 3.3 %all-to-all-start.2 = ((f32[8,1,1024]{2,1,0:T(1,128)}), f32[8,1,1024]{2,1,0:T(1,128)S(1)}, u32[]{:S(2)}, u32[]{:S(2)}) async-start(f32[8,1,1024]{2,1,0:T(1,128)} %reshape.131), calls=%async_computation.2 | async-start | bytes 65536 | tf_op jit(solution)/shard_map/all_to_all | solution.py:126
  59.0 3.0 copy.104
  62.1 3.6 %all-to-all-done.2 = f32[8,1,1024]{2,1,0:T(1,128)S(1)} async-done(((f32[8,1,1024]{2,1,0:T(1,128)}), f32[8,1,1024]{2,1,0:T(1,128)S(1)}, u32[]{:S(2)}, u32[]{:S(2)}) %all-to-all-start.2) | async-done | bytes 32800 | tf_op jit(solution)/shard_map/all_to_all | solution.py:126
  65.7 4.4 %all-to-all-start = ((f32[1,4,256,512]{3,1,0,2:T(4,128)}), f32[1,4,256,512]{3,1,0,2:T(4,128)}, u32[]{:S(2)}, u32[]{:S(2)}) async-start(f32[1,4,256,512]{3,1,0,2:T(4,128)} %copy.104), calls=%async_computation | async-start | bytes 4194304 | tf_op jit(solution)/shard_map/all_to_all | solution.py:127
  74.0 2.6 mul.62
  76.6 4.8 %mul.63 = f32[8,1,4,32,512]{4,3,0,2,1:T(8,128)} reshape(f32[8,4,32,8,64]{4,3,2,0,1:T(8,128)} %mul.62) | data formatting | bytes 4194304 | tf_op jit(solution)/shard_map/mul | solution.py:132
  81.8 34.4 %all-to-all-done = f32[1,4,256,512]{3,1,0,2:T(4,128)} async-done(((f32[1,4,256,512]{3,1,0,2:T(4,128)}), f32[1,4,256,512]{3,1,0,2:T(4,128)}, u32[]{:S(2)}, u32[]{:S(2)}) %all-to-all-start) | async-done | bytes 2097184 | tf_op jit(solution)/shard_map/all_to_all | solution.py:127
  116.1 2.4 copy.79
  120.5 1.9 collective-permute-start
  122.4 1.3 collective-permute-start.1
  123.8 3.1 collective-permute-done.1
  127.7 2.6 add_convert_fusion.1
  130.3 4.5 %collective-permute-start.2 = (bf16[2,32,512]{2,1,0:T(8,128)(2,1)S(1)}, bf16[2,32,512]{2,1,0:T(8,128)(2,1)S(1)}, u32[]{:S(2)}, u32[]{:S(2)}) collective-permute-start(bf16[2,32,512]{2,1,0:T(8,128)(2,1)S(1)} %get-tuple-element.258), channel_id=1, source_target_pairs={{0,1},{1,2},{2,3},{4,5},{5,6},{6,7},{8,9},{9,10},{10,11},{12,13},{... | collective-permute-start | bytes 196616 | tf_op jit(solution)/shard_map/ppermute | solution.py:23
  134.8 1.3 collective-permute-start.3
  138.0 2.6 fusion.88
  140.6 1.3 collective-permute-start.4
  141.9 5.0 %collective-permute-start.5 = (bf16[2,32,512]{2,1,0:T(8,128)(2,1)S(1)}, bf16[2,32,512]{2,1,0:T(8,128)(2,1)S(1)}, u32[]{:S(2)}, u32[]{:S(2)}) collective-permute-start(bf16[2,32,512]{2,1,0:T(8,128)(2,1)S(1)} %get-tuple-element.255), channel_id=1, source_target_pairs={{0,1},{1,2},{2,3},{4,5},{5,6},{6,7},{8,9},{9,10},{10,11},{12,13},{... | collective-permute-start | bytes 196616 | tf_op jit(solution)/shard_map/ppermute | solution.py:23
  148.5 1.3 collective-permute-start.6
  149.8 4.7 %collective-permute-start.7 = (bf16[1,32,512]{2,1,0:T(8,128)(2,1)S(1)}, bf16[1,32,512]{2,1,0:T(8,128)(2,1)S(1)}, u32[]{:S(2)}, u32[]{:S(2)}) collective-permute-start(bf16[1,32,512]{2,1,0:T(8,128)(2,1)S(1)} %get-tuple-element.251), channel_id=1, source_target_pairs={{0,1},{1,2},{2,3},{4,5},{5,6},{6,7},{8,9},{9,10},{10,11},{12,13},{... | collective-permute-start | bytes 98312 | tf_op jit(solution)/shard_map/ppermute | solution.py:23
  157.1 31.8 %all_gather.13 = f32[4,256,8]{2,0,1:T(4,128)S(1)} all-gather(f32[4,32,8]{2,0,1:T(4,128)S(1)} %copy-done.10), channel_id=1, replica_groups=mesh['contacts'=8,'tm'=4] {'contacts'}, dimensions={1}, use_global_device_ids=true | all-gather | bytes 36864 | tf_op jit(solution)/shard_map/all_gather | solution.py:181
  189.2 31.8 %all_gather.12 = f32[4,256,8]{2,0,1:T(4,128)S(1)} all-gather(f32[4,32,8]{2,0,1:T(4,128)S(1)} %copy-done.12), channel_id=1, replica_groups=mesh['contacts'=8,'tm'=4] {'contacts'}, dimensions={1}, use_global_device_ids=true | all-gather | bytes 36864 | tf_op jit(solution)/shard_map/all_gather | solution.py:180
  221.2 1.9 all-gather.3.cloned.1.call-done
  223.2 3.2 %convert_multiply_fusion = f32[4,256,512]{2,1,0:T(8,128)} fusion(bf16[4,256,512]{2,1,0:T(8,128)(2,1)} %all-gather.5.cloned.1.call-done, bf16[4,256,512]{2,1,0:T(8,128)(2,1)} %all-gather.3.cloned.1.call-done), kind=kLoop, calls=%fused_computation.49 | loop fusion | flops 1572864 | bytes 4194304 | tf_op jit(solution)/shard_map/mul | solution.py:184
  226.4 2.9 copy.89
  229.3 1.8 bitcast_reduce_fusion.1
  231.1 24.6 %while.27 = (s32[]{:T(128)}, f32[256,8,64]{0,2,1:T(8,128)}, bf16[2,2,256,2,8,64]{2,5,1,4,3,0:T(8,128)(2,1)S(1)}, bf16[256,8,64]{0,2,1:T(8,128)(2,1)S(1)}, f32[2,...) while((s32[]{:T(128)}, f32[256,8,64]{0,2,1:T(8,128)}, ...), condition=%wide.region_9.10_spmd.clone, body=%wide.region_8.9_spmd.clone.sunk | while | flops 411304192 | bytes 20366760 | solution.py:213
  231.2 2.7 fusion.135
  234.7 2.0 copy.140
  236.8 1.2 iota_compare_fusion.5
  238.0 5.3 %fusion.136 = f32[256,8,64]{0,2,1:T(8,128)} fusion(f32[8,2,256,256]{3,2,1,0:T(8,128)} %fusion.135, f32[2,8,256]{2,0,1:T(2,128)S(1)} %bitcast.306, f32[2,8,256]{2,0,1:T(2,128)S(1)} %get-tuple-element.378, f32[2,8,256]{2,0,1:T(2,128)S(1)} %get-tuple-element.379, pred[256]{0:T(512)(128)(4,1)} %iota_compare_fusion.5, ...), kind=kOutput, calls=%fused_computation.30.clone.1 | convolution fusion | flops 277086208 | bytes 6865921 | tf_op jit(solution)/shard_map/while/body/eval_jaxpr/phic,pche->ihe/dot_general | solution.py:208
  243.4 2.7 fusion.135
  247.0 2.0 copy.140
  249.0 1.2 iota_compare_fusion.5
  250.3 5.4 %fusion.136 = f32[256,8,64]{0,2,1:T(8,128)} fusion(f32[8,2,256,256]{3,2,1,0:T(8,128)} %fusion.135, f32[2,8,256]{2,0,1:T(2,128)S(1)} %bitcast.306, f32[2,8,256]{2,0,1:T(2,128)S(1)} %get-tuple-element.378, f32[2,8,256]{2,0,1:T(2,128)S(1)} %get-tuple-element.379, pred[256]{0:T(512)(128)(4,1)} %iota_compare_fusion.5, ...), kind=kOutput, calls=%fused_computation.30.clone.1 | convolution fusion | flops 277086208 | bytes 6865921 | tf_op jit(solution)/shard_map/while/body/eval_jaxpr/phic,pche->ihe/dot_general | solution.py:208
  255.7 1.2 broadcast_multiply_fusion
  256.9 44.9 %all-reduce.1 = bf16[256,512]{0,1:T(8,128)(2,1)S(1)} all-reduce(f32[256,512]{0,1:T(8,128)S(1)} %bitcast.298), channel_id=1, replica_groups=mesh['contacts'=8,'tm'=4] {'contacts','tm'}, use_global_device_ids=true, to_apply=%region_10.11 | all-reduce | flops 131072 | bytes 786432 | tf_op jit(solution)/shard_map/psum | solution.py:224
  301.8 2.2 fusion.109
  (124 shorter events, 28.6 us)
Async XLA Ops:
  7.2 7.0 %copy-start = (bf16[512,1024]{1,0:T(8,128)(2,1)S(1)}, bf16[512,1024]{1,0:T(8,128)(2,1)}, u32[]{:S(2)}) copy-start(bf16[512,1024]{1,0:T(8,128)(2,1)} %param.22) | copy-start | bytes 3145732
  7.2 6.5 %copy-start.14 = (bf16[32,512]{1,0:T(8,128)(2,1)S(1)}, bf16[32,512]{1,0:T(8,128)(2,1)}, u32[]{:S(2)}) copy-start(bf16[32,512]{1,0:T(8,128)(2,1)} %param.21) | copy-start | bytes 98308
  23.2 4.5 %copy-start.8 = (bf16[512,512]{1,0:T(8,128)(2,1)S(1)}, bf16[512,512]{1,0:T(8,128)(2,1)}, u32[]{:S(2)}) copy-start(bf16[512,512]{1,0:T(8,128)(2,1)} %param.23) | copy-start | bytes 1572868
  23.2 4.6 %copy-start.13 = (bf16[256,512]{1,0:T(8,128)(2,1)S(1)}, bf16[256,512]{1,0:T(8,128)(2,1)}, u32[]{:S(2)}) copy-start(bf16[256,512]{1,0:T(8,128)(2,1)} %param.19) | copy-start | bytes 786436
  31.2 1.6 copy-start.6
  32.9 1.4 copy-start.7
  37.2 1.6 copy-start.6
  38.9 1.4 copy-start.7
  41.7 14.0 %all-to-all-start.1 = ((f32[8,1,1024]{2,1,0:T(1,128)}), f32[8,1,1024]{2,1,0:T(1,128)S(1)}, u32[]{:S(2)}, u32[]{:S(2)}) async-start(f32[8,1,1024]{2,1,0:T(1,128)} %reshape.133), calls=%async_computation.1 | async-start | bytes 65536 | tf_op jit(solution)/shard_map/all_to_all | solution.py:125
  55.7 10.0 %all-to-all-start.2 = ((f32[8,1,1024]{2,1,0:T(1,128)}), f32[8,1,1024]{2,1,0:T(1,128)S(1)}, u32[]{:S(2)}, u32[]{:S(2)}) async-start(f32[8,1,1024]{2,1,0:T(1,128)} %reshape.131), calls=%async_computation.2 | async-start | bytes 65536 | tf_op jit(solution)/shard_map/all_to_all | solution.py:126
  65.7 50.5 %all-to-all-start = ((f32[1,4,256,512]{3,1,0,2:T(4,128)}), f32[1,4,256,512]{3,1,0,2:T(4,128)}, u32[]{:S(2)}, u32[]{:S(2)}) async-start(f32[1,4,256,512]{3,1,0,2:T(4,128)} %copy.104), calls=%async_computation | async-start | bytes 4194304 | tf_op jit(solution)/shard_map/all_to_all | solution.py:127
  70.0 151.2 %all-gather.5.cloned.1.call-start = ((), (), s32[]{:S(2)}) async-start(), calls=%async_computation.4 | async-start | bytes 1179648 | tf_op jit(solution)/shard_map/all_gather | solution.py:177
  73.7 2.9 copy-start.11
  73.9 7.5 %copy-start.9 = (f32[4,32,8]{2,0,1:T(4,128)}, f32[4,32,8]{2,0,1:T(4,128)S(1)}, u32[]{:S(2)}) copy-start(f32[4,32,8]{2,0,1:T(4,128)S(1)} %get-tuple-element.238) | copy-start | bytes 12292
  116.1 2.4 copy-start.3
  118.6 1.0 copy-start.4
  118.6 5.1 %copy-start.15 = (f32[2,512]{1,0:T(2,128)S(1)}, f32[2,512]{1,0:T(2,128)}, u32[]{:S(2)}) copy-start(f32[2,512]{1,0:T(2,128)} %param.26) | copy-start | bytes 12292
  120.5 3.3 %collective-permute-start = (bf16[1,32,512]{2,1,0:T(8,128)(2,1)}, bf16[1,32,512]{2,1,0:T(8,128)(2,1)}, u32[]{:S(2)}, u32[]{:S(2)}) collective-permute-start(bf16[1,32,512]{2,1,0:T(8,128)(2,1)} %get-tuple-element.262), channel_id=1, source_target_pairs={{0,1},{1,2},{2,3},{4,5},{5,6},{6,7},{8,9},{9,10},{10,11},{12,13},{... | collective-permute-start | bytes 98312 | tf_op jit(solution)/shard_map/ppermute | solution.py:23
  122.4 4.6 %collective-permute-start.1 = (bf16[1,32,512]{2,1,0:T(8,128)(2,1)}, bf16[1,32,512]{2,1,0:T(8,128)(2,1)}, u32[]{:S(2)}, u32[]{:S(2)}) collective-permute-start(bf16[1,32,512]{2,1,0:T(8,128)(2,1)} %get-tuple-element.263), channel_id=1, source_target_pairs={{1,0},{2,1},{3,2},{5,4},{6,5},{7,6},{9,8},{10,9},{11,10},{13,12},{... | collective-permute-start | bytes 98312 | tf_op jit(solution)/shard_map/ppermute | solution.py:24
  127.7 10.3 %copy-start.17 = (bf16[4,32,512]{2,1,0:T(8,128)(2,1)S(1)}, bf16[4,32,512]{2,1,0:T(8,128)(2,1)}, u32[]{:S(2)}) copy-start(bf16[4,32,512]{2,1,0:T(8,128)(2,1)} %param.27) | copy-start | bytes 393220
  130.3 6.6 %collective-permute-start.2 = (bf16[2,32,512]{2,1,0:T(8,128)(2,1)S(1)}, bf16[2,32,512]{2,1,0:T(8,128)(2,1)S(1)}, u32[]{:S(2)}, u32[]{:S(2)}) collective-permute-start(bf16[2,32,512]{2,1,0:T(8,128)(2,1)S(1)} %get-tuple-element.258), channel_id=1, source_target_pairs={{0,1},{1,2},{2,3},{4,5},{5,6},{6,7},{8,9},{9,10},{10,11},{12,13},{... | collective-permute-start | bytes 196616 | tf_op jit(solution)/shard_map/ppermute | solution.py:23
  134.8 3.1 %collective-permute-start.3 = (bf16[2,32,512]{2,1,0:T(8,128)(2,1)S(1)}, bf16[2,32,512]{2,1,0:T(8,128)(2,1)S(1)}, u32[]{:S(2)}, u32[]{:S(2)}) collective-permute-start(bf16[2,32,512]{2,1,0:T(8,128)(2,1)S(1)} %get-tuple-element.259), channel_id=1, source_target_pairs={{1,0},{2,1},{3,2},{5,4},{6,5},{7,6},{9,8},{10,9},{11,10},{13,12},{... | collective-permute-start | bytes 196616 | tf_op jit(solution)/shard_map/ppermute | solution.py:24
  136.8 11.0 %copy-start.18 = (f32[4,32,512]{2,1,0:T(8,128)S(1)}, f32[4,32,512]{2,1,0:T(8,128)}, u32[]{:S(2)}) copy-start(f32[4,32,512]{2,1,0:T(8,128)} %get-tuple-element.267) | copy-start | bytes 786436
  136.8 86.3 %all-gather.3.cloned.1.call-start = ((), (), s32[]{:S(2)}) async-start(), calls=%async_computation.3 | async-start | bytes 1179648 | tf_op jit(solution)/shard_map/all_gather | solution.py:176
  136.9 10.9 %copy-start.16 = (bf16[2,3,512,512]{3,2,1,0:T(8,128)(2,1)S(1)}, bf16[2,3,512,512]{3,2,1,0:T(8,128)(2,1)}, u32[]{:S(2)}) copy-start(bf16[2,3,512,512]{3,2,1,0:T(8,128)(2,1)} %param.25) | copy-start | bytes 9437188
  140.6 6.3 %collective-permute-start.4 = (bf16[2,32,512]{2,1,0:T(8,128)(2,1)S(1)}, bf16[2,32,512]{2,1,0:T(8,128)(2,1)S(1)}, u32[]{:S(2)}, u32[]{:S(2)}) collective-permute-start(bf16[2,32,512]{2,1,0:T(8,128)(2,1)S(1)} %get-tuple-element.254), channel_id=1, source_target_pairs={{1,0},{2,1},{3,2},{5,4},{6,5},{7,6},{9,8},{10,9},{11,10},{13,12},{... | collective-permute-start | bytes 196616 | tf_op jit(solution)/shard_map/ppermute | solution.py:24
  141.9 5.9 %collective-permute-start.5 = (bf16[2,32,512]{2,1,0:T(8,128)(2,1)S(1)}, bf16[2,32,512]{2,1,0:T(8,128)(2,1)S(1)}, u32[]{:S(2)}, u32[]{:S(2)}) collective-permute-start(bf16[2,32,512]{2,1,0:T(8,128)(2,1)S(1)} %get-tuple-element.255), channel_id=1, source_target_pairs={{0,1},{1,2},{2,3},{4,5},{5,6},{6,7},{8,9},{9,10},{10,11},{12,13},{... | collective-permute-start | bytes 196616 | tf_op jit(solution)/shard_map/ppermute | solution.py:23
  147.8 8.2 %copy-start.5 = (bf16[512,512]{1,0:T(8,128)(2,1)S(1)}, bf16[512,512]{1,0:T(8,128)(2,1)}, u32[]{:S(2)}) copy-start(bf16[512,512]{1,0:T(8,128)(2,1)} %param.24) | copy-start | bytes 1572868
  148.5 8.6 %copy-start.10 = (f32[4,32,8]{2,0,1:T(4,128)S(1)}, f32[4,32,8]{2,0,1:T(4,128)}, u32[]{:S(2)}) copy-start(f32[4,32,8]{2,0,1:T(4,128)} %copy-done.9) | copy-start | bytes 12292
  148.5 40.7 %copy-start.12 = (f32[4,32,8]{2,0,1:T(4,128)S(1)}, f32[4,32,8]{2,0,1:T(4,128)}, u32[]{:S(2)}) copy-start(f32[4,32,8]{2,0,1:T(4,128)} %copy-done.11) | copy-start | bytes 12292
  148.5 6.0 %collective-permute-start.6 = (bf16[1,32,512]{2,1,0:T(8,128)(2,1)S(1)}, bf16[1,32,512]{2,1,0:T(8,128)(2,1)S(1)}, u32[]{:S(2)}, u32[]{:S(2)}) collective-permute-start(bf16[1,32,512]{2,1,0:T(8,128)(2,1)S(1)} %get-tuple-element.250), channel_id=1, source_target_pairs={{1,0},{2,1},{3,2},{5,4},{6,5},{7,6},{9,8},{10,9},{11,10},{13,12},{... | collective-permute-start | bytes 98312 | tf_op jit(solution)/shard_map/ppermute | solution.py:24
  149.8 5.5 %collective-permute-start.7 = (bf16[1,32,512]{2,1,0:T(8,128)(2,1)S(1)}, bf16[1,32,512]{2,1,0:T(8,128)(2,1)S(1)}, u32[]{:S(2)}, u32[]{:S(2)}) collective-permute-start(bf16[1,32,512]{2,1,0:T(8,128)(2,1)S(1)} %get-tuple-element.251), channel_id=1, source_target_pairs={{0,1},{1,2},{2,3},{4,5},{5,6},{6,7},{8,9},{9,10},{10,11},{12,13},{... | collective-permute-start | bytes 98312 | tf_op jit(solution)/shard_map/ppermute | solution.py:23
  231.1 2.8 copy-start.2
  243.3 2.8 copy-start.2
  255.7 48.3 %copy-start.1 = (bf16[512,1024]{1,0:T(8,128)(2,1)S(1)}, bf16[512,1024]{1,0:T(8,128)(2,1)}, u32[]{:S(2)}) copy-start(bf16[512,1024]{1,0:T(8,128)(2,1)} %param.22) | copy-start | bytes 3145732
Sparse Core Ops, SparseCore 0:
  137.0 42.6 all-gather.4
  181.8 41.2 all-gather.2
where the time goes:
time: 312 us; the launch traced here: 311 us
  blocking collectives  108 us (35%)
  waiting for transfers between devices  51 us (16%)
  local copies, waits for them, and re-layouts  49.8 us (16%)
  starting transfers between devices  36.5 us (12%)
  matrix products  32.4 us (10%)
  other arithmetic  17.9 us (6%)
  between operations  14.6 us (5%)
    psum x1, blocking collectives, local(): lax.psum((dq_sum * scale_dot).reshape(lat_rows, model_width), ('contacts'...  44.9 us
    all_to_all x1, waiting for transfers between devices, local(): lax.all_to_all(accum_out[None], 'contacts', split_axis=2, concat_axis=0,...  34.4 us
    all_gather x1, blocking collectives, local(): lax.all_gather(own_total, 'contacts', axis=1, tiled=True)  31.8 us
    all_gather x1, blocking collectives, local(): lax.all_gather(own_top, 'contacts', axis=1, tiled=True)  31.8 us
    ppermute x4, starting transfers between devices, with_halo(): before = lax.ppermute(last, axis, up)  16.1 us
    dot_general x2, matrix products, back_block(): jnp.einsum('phic,pche->ihe', dscore, key_block, preferred_element_type=jn...  10.7 us
    unnamed x40, local copies, waits for them, and re-layouts  10.2 us
    dot_general x4, matrix products, masked_scores(): jnp.einsum('ihe,pche->phic', queries, key_block, preferred_element_type=j...  7.51 us
  transfers between devices with their start and end apart: 13, of which 8 were waited for; matrix products, arithmetic and copies ran while one was open for 7% of the time, Pallas kernels for 0%

commit v1 on v0

--- a/solution.py
+++ b/solution.py
@@ -1,6 +1,10 @@
+import functools
+
 import jax
 import jax.numpy as jnp
 from jax import lax
+from jax.experimental import pallas as pl
+from jax.experimental.pallas import tpu as pltpu
 from jax.sharding import PartitionSpec as P
 
 HD = 64
@@ -231,6 +235,506 @@
     return (current, d_latents)
 
 
+MESH = pl.DeviceIdType.MESH
+HALO = 3
+CHUNK = 512
+VMEM_CAP = 56 * 1024 * 1024
+
+
+def dot_nn(lhs, rhs):
+    return jnp.dot(lhs, rhs, preferred_element_type=jnp.float32)
+
+
+def dot_nt(lhs, rhs):
+    return lax.dot_general(lhs, rhs, (((1,), (1,)), ((), ())), preferred_element_type=jnp.float32)
+
+
+def fused_kernel(
+    groups,
+    times,
+    sig_ref,
+    idx_ref,
+    latents_ref,
+    w_in_ref,
+    w_query_ref,
+    bias_ref,
+    cot_ref,
+    table_hbm,
+    w_kv_hbm,
+    w_out_hbm,
+    conv_hbm,
+    feat_ref,
+    dlat_ref,
+    table_ref,
+    w_kv_ref,
+    w_out_ref,
+    conv_ref,
+    sig_all,
+    idx_all,
+    w_wide,
+    pos_rows,
+    valid_ref,
+    kv_ref,
+    exp_ref,
+    prob_ref,
+    inv_tot,
+    q_wide,
+    att_ref,
+    cot_halo,
+    x_ext,
+    g_ext,
+    gpre_ref,
+    g1_ref,
+    dq_acc,
+    dq_parts,
+    dq_all,
+    load_sem,
+    idx_send,
+    idx_recv,
+    sig_send,
+    sig_recv,
+    halo_send,
+    halo_recv,
+    part_send,
+    part_recv,
+    all_send,
+    all_recv,
+):
+    me = lax.axis_index("contacts")
+    tm = lax.axis_index("tm")
+    con_dev, width_sig = sig_ref.shape
+    pat_dev = width_sig // PATCH
+    lat_dev, width = att_ref.shape[1:]
+    heads = width // HD
+    rows = heads * lat_dev
+    contacts = groups * con_dev
+    table_rows = table_ref.shape[0]
+
+    loads = [
+        pltpu.make_async_copy(src, dst, load_sem.at[n])
+        for n, (src, dst) in enumerate(
+            (
+                (table_hbm, table_ref),
+                (w_kv_hbm, w_kv_ref),
+                (w_out_hbm, w_out_ref),
+                (conv_hbm, conv_ref),
+            )
+        )
+    ]
+    for load in loads:
+        load.start()
+
+    barrier = pltpu.get_barrier_semaphore()
+    for k in range(1, groups):
+        pl.semaphore_signal(
+            barrier, inc=1, device_id=(lax.rem(me + k, groups), tm), device_id_type=MESH
+        )
+    for k in range(1, times):
+        pl.semaphore_signal(
+            barrier, inc=1, device_id=(me, lax.rem(tm + k, times)), device_id_type=MESH
+        )
+    pl.semaphore_wait(barrier, groups + times - 2)
+
+    def remote(src, dst, send, recv, contact_id, tm_id):
+        return pltpu.make_async_remote_copy(
+            src_ref=src,
+            dst_ref=dst,
+            send_sem=send,
+            recv_sem=recv,
+            device_id=(contact_id, tm_id),
+            device_id_type=MESH,
+        )
+
+    def idx_copy(k):
+        return remote(
+            idx_ref, idx_all.at[me], idx_send.at[k], idx_recv.at[k], lax.rem(me + k, groups), tm
+        )
+
+    def sig_copy(k):
+        return remote(
+            sig_ref, sig_all.at[me], sig_send.at[k], sig_recv.at[k], lax.rem(me + k, groups), tm
+        )
+
+    def to_right(src, dst, n):
+        return remote(src, dst, halo_send.at[n], halo_recv.at[n], me, tm + 1)
+
+    def to_left(src, dst, n):
+        return remote(src, dst, halo_send.at[n], halo_recv.at[n], me, tm - 1)
+
+    has_left = tm > 0
+    has_right = tm < times - 1
+
+    cot_pair = (
+        to_right(cot_ref.at[pl.ds(pat_dev - 1, 1)], cot_halo.at[pl.ds(0, 1)], 0),
+        to_left(cot_ref.at[pl.ds(0, 1)], cot_halo.at[pl.ds(1, 1)], 1),
+    )
+
+    def ext_pair(ext, n):
+        return (
+            to_right(ext.at[pl.ds(pat_dev, HALO)], ext.at[pl.ds(0, HALO)], n),
+            to_left(ext.at[pl.ds(HALO, HALO)], ext.at[pl.ds(HALO + pat_dev, HALO)], n + 1),
+        )
+
+    x_pair = ext_pair(x_ext, 2)
+    g_pair = ext_pair(g_ext, 4)
+
+    def start_pair(pair):
+        @pl.when(has_right)
+        def _():
+            pair[0].start()
+
+        @pl.when(has_left)
+        def _():
+            pair[1].start()
+
+    def arrive_pair(pair):
+        @pl.when(has_left)
+        def _():
+            pair[0].wait_recv()
+
+        @pl.when(has_right)
+        def _():
+            pair[1].wait_recv()
+
+    def sent_pair(pair):
+        @pl.when(has_right)
+        def _():
+            pair[0].wait_send()
+
+        @pl.when(has_left)
+        def _():
+            pair[1].wait_send()
+
+    for k in range(1, groups):
+        idx_copy(k).start()
+    for k in range(1, groups):
+        sig_copy(k).start()
+    start_pair(cot_pair)
+
+    @pl.when(jnp.logical_not(has_left))
+    def _():
+        x_ext[0:HALO] = jnp.zeros((HALO, lat_dev, width), jnp.bfloat16)
+        g_ext[0:HALO] = jnp.zeros((HALO, lat_dev, width), jnp.bfloat16)
+        cot_halo[0:1] = jnp.zeros((1, lat_dev, width), jnp.bfloat16)
+
+    @pl.when(jnp.logical_not(has_right))
+    def _():
+        x_ext[HALO + pat_dev :] = jnp.zeros((HALO, lat_dev, width), jnp.bfloat16)
+        g_ext[HALO + pat_dev :] = jnp.zeros((HALO, lat_dev, width), jnp.bfloat16)
+        cot_halo[1:2] = jnp.zeros((1, lat_dev, width), jnp.bfloat16)
+
+    idx_all[me] = idx_ref[...]
+    sig_all[me] = sig_ref[...]
+
+    for p in range(pat_dev):
+        w_wide[p] = jnp.zeros((width_sig, width), jnp.bfloat16)
+        w_wide[p, p * PATCH : (p + 1) * PATCH, :] = w_in_ref[...]
+
+    own_head = (
+        lax.broadcasted_iota(jnp.int32, (rows, width), 0) // lat_dev
+        == lax.broadcasted_iota(jnp.int32, (rows, width), 1) // HD
+    )
+
+    def widen(values):
+        return jnp.where(own_head, jnp.concatenate([values] * heads, axis=0), 0.0)
+
+    def narrow(values):
+        return jnp.sum(jnp.where(own_head, values, 0.0).reshape(heads, lat_dev, width), axis=0)
+
+    own_latents = latents_ref[pl.ds(pl.multiple_of(me * lat_dev, lat_dev), lat_dev), :]
+    queries = dot_nn(own_latents, w_query_ref[...]).astype(jnp.bfloat16).astype(jnp.float32)
+    q_wide[...] = widen(queries * scale_dot).astype(jnp.bfloat16)
+
+    loads[0].wait()
+
+    def gather_block(k, carry):
+        @pl.when(k > 0)
+        def _():
+            idx_copy(k).wait_recv()
+
+        block = lax.rem(me - k + groups, groups)
+        idx_rows = idx_all[block]
+        start = pl.multiple_of(block * con_dev, con_dev)
+        valid_ref[:, pl.ds(start, con_dev)] = jnp.where(idx_rows >= 0, 1.0, 0.0)
+        column = jnp.transpose(
+            jnp.broadcast_to(idx_rows[0:1].astype(jnp.float32), (128, con_dev))
+        ).astype(jnp.int32)[:, 0:1]
+        total = jnp.zeros((con_dev, width), jnp.float32)
+        for first in range(0, table_rows, CHUNK):
+            spots = lax.broadcasted_iota(jnp.int32, (con_dev, CHUNK), 1) + first
+            hot = jnp.where(column == spots, 1.0, 0.0).astype(jnp.bfloat16)
+            total += dot_nn(hot, table_ref[first : first + CHUNK, :])
+        pos_rows[block] = total.astype(jnp.bfloat16)
+        return carry
+
+    lax.fori_loop(0, groups, gather_block, 0)
+    loads[1].wait()
+
+    def project_block(k, carry):
+        @pl.when(k > 0)
+        def _():
+            sig_copy(k).wait_recv()
+
+        block = lax.rem(me - k + groups, groups)
+        sig_block = sig_all[block]
+        pos_block = pos_rows[block].astype(jnp.float32)
+        start = pl.multiple_of(block * con_dev, con_dev)
+        for p in range(pat_dev):
+            tokens = (dot_nn(sig_block, w_wide[p]) + pos_block).astype(jnp.bfloat16)
+            kv_ref[p, pl.ds(start, con_dev), :] = dot_nn(tokens, w_kv_ref[...]).astype(
+                jnp.bfloat16
+            )
+        return carry
+
+    lax.fori_loop(0, groups, project_block, 0)
+
+    def forward(p, carry):
+        top = jnp.full((rows, 1), neg_big, jnp.float32)
+        for first in range(0, contacts, CHUNK):
+            scores = dot_nt(q_wide[...], kv_ref[p, first : first + CHUNK, 0:width])
+            scores = jnp.where(valid_ref[0:1, first : first + CHUNK] > 0.0, scores, neg_big)
+            exp_ref[p, :, first : first + CHUNK] = scores
+            top = jnp.maximum(top, jnp.max(scores, axis=1, keepdims=True))
+        totals = jnp.zeros((rows, 1), jnp.float32)
+        for first in range(0, contacts, CHUNK):
+            weights = jnp.where(
+                valid_ref[0:1, first : first + CHUNK] > 0.0,
+                jnp.exp(exp_ref[p, :, first : first + CHUNK] - top),
+                0.0,
+            )
+            exp_ref[p, :, first : first + CHUNK] = weights
+            prob_ref[:, first : first + CHUNK] = weights.astype(jnp.bfloat16)
+            totals += jnp.sum(weights, axis=1, keepdims=True)
+        mixed = dot_nn(prob_ref[...], kv_ref[p, :, width : 2 * width])
+        inv_tot[p] = jnp.broadcast_to(1.0 / totals, (rows, 128))
+        att_ref[p] = narrow(mixed / totals).astype(jnp.bfloat16)
+        return carry
+
+    lax.fori_loop(0, pat_dev, forward, 0)
+    loads[2].wait()
+    loads[3].wait()
+
+    def flat(values):
+        return values.reshape(values.shape[0] * lat_dev, width)
+
+    x_own = dot_nn(flat(att_ref[...]), w_out_ref[...]).astype(jnp.bfloat16)
+    x_ext[HALO : HALO + pat_dev] = x_own.reshape(pat_dev, lat_dev, width)
+    start_pair(x_pair)
+    arrive_pair(x_pair)
+    arrive_pair(cot_pair)
+
+    def inside(count, before):
+        window = (
+            lax.broadcasted_iota(jnp.int32, (count * lat_dev, width), 0) // lat_dev
+            + tm * pat_dev
+            - before
+        )
+        return jnp.logical_and(window >= 0, window < times * pat_dev)
+
+    wide0 = pat_dev + 4
+    pre0 = bias_ref[0:1, :]
+    for j in range(KSIZE):
+        pre0 = pre0 + dot_nn(flat(x_ext[j : j + wide0]), conv_ref[0, j])
+    x1 = flat(x_ext[1 : 1 + wide0]).astype(jnp.float32) + pre0 * jax.nn.sigmoid(pre0)
+    x1 = jnp.where(inside(wide0, 2), x1, 0.0).astype(jnp.bfloat16)
+    pre1 = bias_ref[1:2, :]
+    span = pat_dev * lat_dev
+    for j in range(KSIZE):
+        first = 2 * j * lat_dev
+        pre1 = pre1 + dot_nn(x1[first : first + span], conv_ref[1, j])
+    first = 2 * lat_dev
+    x2 = x1[first : first + span].astype(jnp.float32) + pre1 * jax.nn.sigmoid(pre1)
+    feat_ref[...] = x2.astype(jnp.bfloat16).reshape(pat_dev, lat_dev, width)
+
+    cot_own = flat(cot_ref[...]).astype(jnp.float32)
+    gpre1 = (cot_own * silu_slope(pre1)).astype(jnp.bfloat16)
+    g_ext[HALO : HALO + pat_dev] = gpre1.reshape(pat_dev, lat_dev, width)
+    start_pair(g_pair)
+    arrive_pair(g_pair)
+
+    wide1 = pat_dev + 2
+    g1 = jnp.concatenate(
+        [cot_halo[0].astype(jnp.float32), cot_own, cot_halo[1].astype(jnp.float32)], axis=0
+    )
+    for j in range(KSIZE):
+        g1 = g1 + dot_nt(flat(g_ext[4 - 2 * j : 4 - 2 * j + wide1]), conv_ref[1, j])
+    gpre0 = g1 * silu_slope(pre0[lat_dev : lat_dev + wide1 * lat_dev])
+    gpre0 = jnp.where(inside(wide1, 1), gpre0, 0.0).astype(jnp.bfloat16)
+    gpre_ref[...] = gpre0.reshape(wide1, lat_dev, width)
+    g1_ref[...] = g1
+    g0 = dot_nt(flat(gpre_ref[2 : 2 + pat_dev]), conv_ref[0, 0])
+    for j in range(1, KSIZE):
+        g0 = g0 + dot_nt(flat(gpre_ref[2 - j : 2 - j + pat_dev]), conv_ref[0, j])
+    g0 = g0 + g1_ref[lat_dev : lat_dev + span]
+    grad_att = dot_nt(g0.astype(jnp.bfloat16), w_out_ref[...]).astype(jnp.bfloat16)
+    sent_pair(x_pair)
+    x_ext[HALO : HALO + pat_dev] = grad_att.reshape(pat_dev, lat_dev, width)
+
+    dq_acc[...] = jnp.zeros((rows, width), jnp.float32)
+
+    def backward(p, carry):
+        grad_wide = widen(x_ext[HALO + p].astype(jnp.float32))
+        att_wide = jnp.concatenate([att_ref[p].astype(jnp.float32)] * heads, axis=0)
+        delta = jnp.sum(grad_wide * att_wide, axis=1, keepdims=True)
+        grad_wide = grad_wide.astype(jnp.bfloat16)
+        scale = inv_tot[p][:, 0:1]
+        for first in range(0, contacts, CHUNK):
+            grad_prob = dot_nt(grad_wide, kv_ref[p, first : first + CHUNK, width : 2 * width])
+            prob = exp_ref[p, :, first : first + CHUNK] * scale
+            prob_ref[:, first : first + CHUNK] = (prob * (grad_prob - delta)).astype(jnp.bfloat16)
+        dq_acc[...] += dot_nn(prob_ref[...], kv_ref[p, :, 0:width])
+        return carry
+
+    lax.fori_loop(0, pat_dev, backward, 0)
+
+    dq_parts[tm] = narrow(dq_acc[...]) * scale_dot
+
+    def part_copy(k):
+        return remote(
+            dq_parts.at[tm],
+            dq_parts.at[tm],
+            part_send.at[k],
+            part_recv.at[k],
+            me,
+            lax.rem(tm + k, times),
+        )
+
+    own_rows = pl.ds(pl.multiple_of(me * lat_dev, lat_dev), lat_dev)
+
+    def all_copy(k):
+        return remote(
+            dq_all.at[own_rows],
+            dq_all.at[own_rows],
+            all_send.at[k],
+            all_recv.at[k],
+            lax.rem(me + k, groups),
+            tm,
+        )
+
+    for k in range(1, times):
+        part_copy(k).start()
+    for k in range(1, times):
+        part_copy(k).wait_recv()
+    dq_sum = dq_parts[0]
+    for t in range(1, times):
+        dq_sum = dq_sum + dq_parts[t]
+    dq_all[own_rows, :] = dq_sum.astype(jnp.bfloat16)
+    for k in range(1, groups):
+        all_copy(k).start()
+    for k in range(1, groups):
+        all_copy(k).wait_recv()
+    dlat_ref[...] = dot_nt(dq_all[...], w_query_ref[...])
+
+    for k in range(1, groups):
+        idx_copy(k).wait_send()
+        sig_copy(k).wait_send()
+        all_copy(k).wait_send()
+    for k in range(1, times):
+        part_copy(k).wait_send()
+    sent_pair(cot_pair)
+    sent_pair(g_pair)
+
+
+def fused(
+    signal,
+    pos_idx,
+    live_count,
+    latents,
+    pos_table,
+    w_in,
+    w_kv,
+    w_query,
+    w_out,
+    conv_weight,
+    conv_bias,
+    cotangent,
+):
+    con_dev, width_sig = signal.shape
+    pat_dev = width_sig // PATCH
+    groups, times = lax.axis_size("contacts"), lax.axis_size("tm")
+    lat_rows, width = latents.shape
+    lat_dev = lat_rows // groups
+    rows = width // HD * lat_dev
+    contacts = groups * con_dev
+    is_valid = jnp.arange(con_dev, dtype=jnp.int32) < live_count[0]
+    spots = jnp.broadcast_to(jnp.where(is_valid, pos_idx, -1)[None], (8, con_dev))
+    bf16, f32 = jnp.bfloat16, jnp.float32
+    vmem = pl.BlockSpec(memory_space=pltpu.VMEM)
+    away = pl.BlockSpec(memory_space=pl.ANY)
+    dma = pltpu.SemaphoreType.DMA
+    return pl.pallas_call(
+        functools.partial(fused_kernel, groups, times),
+        out_shape=(
+            jax.ShapeDtypeStruct((pat_dev, lat_dev, width), bf16),
+            jax.ShapeDtypeStruct((lat_rows, width), f32),
+        ),
+        in_specs=[vmem] * 7 + [away] * 4,
+        out_specs=(vmem, vmem),
+        scratch_shapes=[
+            pltpu.VMEM(pos_table.shape, bf16),
+            pltpu.VMEM(w_kv.shape, bf16),
+            pltpu.VMEM(w_out.shape, bf16),
+            pltpu.VMEM(conv_weight.shape, bf16),
+            pltpu.VMEM((groups, con_dev, width_sig), bf16),
+            pltpu.VMEM((groups, 8, con_dev), jnp.int32),
+            pltpu.VMEM((pat_dev, width_sig, width), bf16),
+            pltpu.VMEM((groups, con_dev, width), bf16),
+            pltpu.VMEM((8, contacts), f32),
+            pltpu.VMEM((pat_dev, contacts, 2 * width), bf16),
+            pltpu.VMEM((pat_dev, rows, contacts), f32),
+            pltpu.VMEM((rows, contacts), bf16),
+            pltpu.VMEM((pat_dev, rows, 128), f32),
+            pltpu.VMEM((rows, width), bf16),
+            pltpu.VMEM((pat_dev, lat_dev, width), bf16),
+            pltpu.VMEM((2, lat_dev, width), bf16),
+            pltpu.VMEM((pat_dev + 2 * HALO, lat_dev, width), bf16),
+            pltpu.VMEM((pat_dev + 2 * HALO, lat_dev, width), bf16),
+            pltpu.VMEM((pat_dev + 2, lat_dev, width), bf16),
+            pltpu.VMEM(((pat_dev + 2) * lat_dev, width), f32),
+            pltpu.VMEM((rows, width), f32),
+            pltpu.VMEM((times, lat_dev, width), f32),
+            pltpu.VMEM((lat_rows, width), bf16),
+            dma((4,)),
+            dma((groups,)),
+            dma((groups,)),
+            dma((groups,)),
+            dma((groups,)),
+            dma((6,)),
+            dma((6,)),
+            dma((times,)),
+            dma((times,)),
+            dma((groups,)),
+            dma((groups,)),
+        ],
+        compiler_params=pltpu.CompilerParams(
+            collective_id=0, has_side_effects=True, vmem_limit_bytes=VMEM_CAP
+        ),
+    )(
+        signal,
+        spots,
+        latents,
+        w_in,
+        w_query,
+        conv_bias,
+        cotangent,
+        pos_table,
+        w_kv,
+        w_out,
+        conv_weight,
+    )
+
+
+def device_program(*args):
+    signal, latents = args[0], args[3]
+    groups = lax.axis_size("contacts")
+    pat_dev = signal.shape[1] // PATCH
+    lat_dev = latents.shape[0] // groups
+    held = groups * signal.shape[0] * pat_dev * latents.shape[1] * 4
+    if lat_dev % 16 == 0 and pat_dev >= HALO and held <= 24 * 1024 * 1024:
+        return fused(*args)
+    return local(*args)
+
+
 def solution(mesh):
     in_specs = (
         P("contacts", "tm"),
@@ -247,4 +751,6 @@
         P("tm", "contacts", None),
     )
     out_specs = (P("tm", "contacts", None), P())
-    return jax.shard_map(local, mesh=mesh, in_specs=in_specs, out_specs=out_specs, check_vma=False)
+    return jax.shard_map(
+        device_program, mesh=mesh, in_specs=in_specs, out_specs=out_specs, check_vma=False
+    )

time: 312 us -> 74.8 us (0.24)
  blocking collectives: 108 us -> 0 us
  Pallas kernels: 0 us -> 68.6 us
  waiting for transfers between devices: 51 us -> 0 us
  local copies, waits for them, and re-layouts: 49.8 us -> 4.04 us
  starting transfers between devices: 36.5 us -> 0 us
  matrix products: 32.4 us -> 0 us
  other arithmetic: 17.9 us -> 0.68 us
  between operations: 14.6 us -> 1.29 us
    pallas_call x0 -> x1, Pallas kernels: none -> 68.6 us  [fused(): pl.pallas_call(functools.partial(fused_kernel, groups, times), out_shape=...]
    all_gather x2 -> x0, blocking collectives: 63.6 us -> none  [the longest x1 31.8 us: local(): lax.all_gather(own_total, 'contacts', axis=1, tiled=True)]
    psum x1 -> x0, blocking collectives: 44.9 us -> none  [local(): lax.psum((dq_sum * scale_dot).reshape(lat_rows, model_width), ('contacts'...]
    all_to_all x3 -> x0, waiting for transfers between devices: 43.2 us -> none  [the longest x1 34.4 us: local(): lax.all_to_all(accum_out[None], 'contacts', split_axis=2, concat_axis=0,...]
    dot_general x18 -> x0, matrix products: 32.4 us -> none  [the longest x2 10.7 us: back_block(): jnp.einsum('phic,pche->ihe', dscore, key_block, preferred_element_type=jn...]
    ppermute x8 -> x0, starting transfers between devices: 21.2 us -> none  [the longest x4 16.1 us: with_halo(): before = lax.ppermute(last, axis, up)]
    all_to_all x3 -> x0, starting transfers between devices: 15 us -> none  [the longest x1 7.28 us: local(): lax.all_to_all(top_score[None], 'contacts', split_axis=2, concat_axis=0,...]
    mul x3 -> x0, local copies, waits for them, and re-layouts: 10.3 us -> none  [the longest x2 7.38 us: local(): split_heads(got_acc, head_count) * factor[..., None]]
  transfers between devices with their start and end apart: 13 -> 0, of which waited for: 8 -> 0; matrix products, arithmetic and copies ran while one was open for 7% -> 0% of each run, Pallas kernels for 0% -> 0%
where the time goes in v1:
time: 74.8 us; the launch traced here: 74.6 us
  Pallas kernels  68.6 us (92%)
  local copies, waits for them, and re-layouts  4.04 us (5%)
  between operations  1.29 us (2%)
    pallas_call x1, Pallas kernels, fused(): pl.pallas_call(functools.partial(fused_kernel, groups, times), out_shape=...  68.6 us
    unnamed x2, local copies, waits for them, and re-layouts  3.44 us

profile of v1, /device:TPU:0, one launch (start us, length us, event | category | flops | bytes accessed | tf_op | source)
XLA Modules:
  0.0 74.6 jit_solution(14549993354310859933)
XLA Ops:
  1.3 0.7 compare_select_fusion
  2.0 0.6 broadcast_in_dim.11.idx_ref
  2.6 68.6 %shard_map.131 = (bf16[4,32,512]{2,1,0:T(8,128)(2,1)}, f32[256,512]{1,0:T(8,128)}) custom-call(bf16[256,128]{1,0:T(8,128)(2,1)} %sig_ref.1, s32[8,256]{1,0:T(8,128)} %broadcast_in_dim.11.idx_ref, bf16[256,512]{1,0:T(8,128)(2,1)} %latents_ref.1, bf16[32,512]{1,0:T(8,128)(2,1)} %w_in_ref.1, bf16[512,512]{1,0:T(8,128)(2,1)} %w_query_ref.1, f32[2,512]{1,0:T(2,128)} %bias_ref.1, ...), custom_call_target="tpu_custom_call" | custom-call | tf_op jit(solution)/shard_map/pallas_call | solution.py:665
  71.2 1.6 %copy.17 = bf16[4,32,512]{2,1,0:T(8,128)(2,1)} copy(bf16[4,32,512]{2,1,0:T(8,128)(2,1)} %get-tuple-element.4) | data formatting | bytes 262144
  72.7 1.9 %copy.18 = f32[256,512]{1,0:T(8,128)} copy(f32[256,512]{1,0:T(8,128)} %get-tuple-element.5) | data formatting | bytes 1048576

commit v2 on v1

--- a/solution.py
+++ b/solution.py
@@ -293,6 +293,8 @@
     idx_recv,
     sig_send,
     sig_recv,
+    pos_send,
+    pos_recv,
     halo_send,
     halo_recv,
     part_send,
@@ -447,15 +449,31 @@
 
     loads[0].wait()
 
-    def gather_block(k, carry):
-        @pl.when(k > 0)
-        def _():
-            idx_copy(k).wait_recv()
-
+    core = lax.rem(tm, 2)
+    sibling = tm + 1 - 2 * core
+
+    def pos_copy(k):
+        block = lax.rem(me - k + groups, groups)
+        return remote(
+            pos_rows.at[block], pos_rows.at[block], pos_send.at[k], pos_recv.at[k], me, sibling
+        )
+
+    def mark_valid(k):
+        block = lax.rem(me - k + groups, groups)
+        start = pl.multiple_of(block * con_dev, con_dev)
+        valid_ref[:, pl.ds(start, con_dev)] = jnp.where(idx_all[block] >= 0, 1.0, 0.0)
+
+    def gather_block(pair, carry):
+        @pl.when(pair > 0)
+        def _():
+            idx_copy(2 * pair).wait_recv()
+
+        idx_copy(2 * pair + 1).wait_recv()
+        mark_valid(2 * pair)
+        mark_valid(2 * pair + 1)
+        k = 2 * pair + core
         block = lax.rem(me - k + groups, groups)
         idx_rows = idx_all[block]
-        start = pl.multiple_of(block * con_dev, con_dev)
-        valid_ref[:, pl.ds(start, con_dev)] = jnp.where(idx_rows >= 0, 1.0, 0.0)
         column = jnp.transpose(
             jnp.broadcast_to(idx_rows[0:1].astype(jnp.float32), (128, con_dev))
         ).astype(jnp.int32)[:, 0:1]
@@ -465,15 +483,20 @@
             hot = jnp.where(column == spots, 1.0, 0.0).astype(jnp.bfloat16)
             total += dot_nn(hot, table_ref[first : first + CHUNK, :])
         pos_rows[block] = total.astype(jnp.bfloat16)
+        pos_copy(k).start()
         return carry
 
-    lax.fori_loop(0, groups, gather_block, 0)
+    lax.fori_loop(0, groups // 2, gather_block, 0)
     loads[1].wait()
 
     def project_block(k, carry):
         @pl.when(k > 0)
         def _():
             sig_copy(k).wait_recv()
+
+        @pl.when(lax.rem(k, 2) != core)
+        def _():
+            pos_copy(k).wait_recv()
 
         block = lax.rem(me - k + groups, groups)
         sig_block = sig_all[block]
@@ -497,11 +520,7 @@
             top = jnp.maximum(top, jnp.max(scores, axis=1, keepdims=True))
         totals = jnp.zeros((rows, 1), jnp.float32)
         for first in range(0, contacts, CHUNK):
-            weights = jnp.where(
-                valid_ref[0:1, first : first + CHUNK] > 0.0,
-                jnp.exp(exp_ref[p, :, first : first + CHUNK] - top),
-                0.0,
-            )
+            weights = jnp.exp(exp_ref[p, :, first : first + CHUNK] - top)
             exp_ref[p, :, first : first + CHUNK] = weights
             prob_ref[:, first : first + CHUNK] = weights.astype(jnp.bfloat16)
             totals += jnp.sum(weights, axis=1, keepdims=True)
@@ -629,6 +648,8 @@
         idx_copy(k).wait_send()
         sig_copy(k).wait_send()
         all_copy(k).wait_send()
+    for pair in range(groups // 2):
+        pos_copy(2 * pair + core).wait_send()
     for k in range(1, times):
         part_copy(k).wait_send()
     sent_pair(cot_pair)
@@ -699,6 +720,8 @@
             dma((groups,)),
             dma((groups,)),
             dma((groups,)),
+            dma((groups,)),
+            dma((groups,)),
             dma((6,)),
             dma((6,)),
             dma((times,)),
@@ -730,7 +753,8 @@
     pat_dev = signal.shape[1] // PATCH
     lat_dev = latents.shape[0] // groups
     held = groups * signal.shape[0] * pat_dev * latents.shape[1] * 4
-    if lat_dev % 16 == 0 and pat_dev >= HALO and held <= 24 * 1024 * 1024:
+    paired = groups % 2 == 0 and lax.axis_size("tm") % 2 == 0
+    if paired and lat_dev % 16 == 0 and pat_dev >= HALO and held <= 24 * 1024 * 1024:
         return fused(*args)
     return local(*args)
 

time: 74.8 us -> 72 us (0.963)
  Pallas kernels: 68.6 us -> 65.8 us
    pallas_call x1, Pallas kernels: 68.6 us -> 65.8 us  [fused(): pl.pallas_call(functools.partial(fused_kernel, groups, times), out_shape=...]
where the time goes in v2:
time: 72 us; the launch traced here: 71.8 us
  Pallas kernels  65.8 us (91%)
  local copies, waits for them, and re-layouts  4.04 us (6%)
  between operations  1.29 us (2%)
    pallas_call x1, Pallas kernels, fused(): pl.pallas_call(functools.partial(fused_kernel, groups, times), out_shape=...  65.8 us
    unnamed x2, local copies, waits for them, and re-layouts  3.44 us

profile of v2, /device:TPU:0, one launch (start us, length us, event | category | flops | bytes accessed | tf_op | source)
XLA Modules:
  0.0 71.8 jit_solution(13057759434099541891)
XLA Ops:
  1.3 0.7 compare_select_fusion
  2.0 0.6 broadcast_in_dim.11.idx_ref
  2.6 65.8 %shard_map.131 = (bf16[4,32,512]{2,1,0:T(8,128)(2,1)}, f32[256,512]{1,0:T(8,128)}) custom-call(bf16[256,128]{1,0:T(8,128)(2,1)} %sig_ref.1, s32[8,256]{1,0:T(8,128)} %broadcast_in_dim.11.idx_ref, bf16[256,512]{1,0:T(8,128)(2,1)} %latents_ref.1, bf16[32,512]{1,0:T(8,128)(2,1)} %w_in_ref.1, bf16[512,512]{1,0:T(8,128)(2,1)} %w_query_ref.1, f32[2,512]{1,0:T(2,128)} %bias_ref.1, ...), custom_call_target="tpu_custom_call" | custom-call | tf_op jit(solution)/shard_map/pallas_call | solution.py:686
  68.3 1.6 %copy.17 = bf16[4,32,512]{2,1,0:T(8,128)(2,1)} copy(bf16[4,32,512]{2,1,0:T(8,128)(2,1)} %get-tuple-element.4) | data formatting | bytes 262144
  69.9 1.9 %copy.18 = f32[256,512]{1,0:T(8,128)} copy(f32[256,512]{1,0:T(8,128)} %get-tuple-element.5) | data formatting | bytes 1048576

commit v3 on v2

--- a/solution.py
+++ b/solution.py
@@ -522,14 +522,15 @@
         for first in range(0, contacts, CHUNK):
             weights = jnp.exp(exp_ref[p, :, first : first + CHUNK] - top)
             exp_ref[p, :, first : first + CHUNK] = weights
-            prob_ref[:, first : first + CHUNK] = weights.astype(jnp.bfloat16)
+            prob_ref[p, :, first : first + CHUNK] = weights.astype(jnp.bfloat16)
             totals += jnp.sum(weights, axis=1, keepdims=True)
-        mixed = dot_nn(prob_ref[...], kv_ref[p, :, width : 2 * width])
+        mixed = dot_nn(prob_ref[p], kv_ref[p, :, width : 2 * width])
         inv_tot[p] = jnp.broadcast_to(1.0 / totals, (rows, 128))
         att_ref[p] = narrow(mixed / totals).astype(jnp.bfloat16)
         return carry
 
-    lax.fori_loop(0, pat_dev, forward, 0)
+    for p in range(pat_dev):
+        forward(p, 0)
     loads[2].wait()
     loads[3].wait()
 
@@ -600,11 +601,12 @@
         for first in range(0, contacts, CHUNK):
             grad_prob = dot_nt(grad_wide, kv_ref[p, first : first + CHUNK, width : 2 * width])
             prob = exp_ref[p, :, first : first + CHUNK] * scale
-            prob_ref[:, first : first + CHUNK] = (prob * (grad_prob - delta)).astype(jnp.bfloat16)
-        dq_acc[...] += dot_nn(prob_ref[...], kv_ref[p, :, 0:width])
+            prob_ref[p, :, first : first + CHUNK] = (prob * (grad_prob - delta)).astype(jnp.bfloat16)
+        dq_acc[...] += dot_nn(prob_ref[p], kv_ref[p, :, 0:width])
         return carry
 
-    lax.fori_loop(0, pat_dev, backward, 0)
+    for p in range(pat_dev):
+        backward(p, 0)
 
     dq_parts[tm] = narrow(dq_acc[...]) * scale_dot
 
@@ -703,7 +705,7 @@
             pltpu.VMEM((8, contacts), f32),
             pltpu.VMEM((pat_dev, contacts, 2 * width), bf16),
             pltpu.VMEM((pat_dev, rows, contacts), f32),
-            pltpu.VMEM((rows, contacts), bf16),
+            pltpu.VMEM((pat_dev, rows, contacts), bf16),
             pltpu.VMEM((pat_dev, rows, 128), f32),
             pltpu.VMEM((rows, width), bf16),
             pltpu.VMEM((pat_dev, lat_dev, width), bf16),

time: 72 us -> 70.6 us (0.981)
  Pallas kernels: 65.8 us -> 64.3 us
    pallas_call x1, Pallas kernels: 65.8 us -> 64.3 us  [fused(): pl.pallas_call(functools.partial(fused_kernel, groups, times), out_shape=...]
where the time goes in v3:
time: 70.6 us; the launch traced here: 70.3 us
  Pallas kernels  64.3 us (91%)
  local copies, waits for them, and re-layouts  4.04 us (6%)
  between operations  1.29 us (2%)
    pallas_call x1, Pallas kernels, fused(): pl.pallas_call(functools.partial(fused_kernel, groups, times), out_shape=...  64.3 us
    unnamed x2, local copies, waits for them, and re-layouts  3.44 us

profile of v3, /device:TPU:0, one launch (start us, length us, event | category | flops | bytes accessed | tf_op | source)
XLA Modules:
  0.0 70.3 jit_solution(4327841402431127576)
XLA Ops:
  1.3 0.7 compare_select_fusion
  2.0 0.6 broadcast_in_dim.11.idx_ref
  2.6 64.3 %shard_map.131 = (bf16[4,32,512]{2,1,0:T(8,128)(2,1)}, f32[256,512]{1,0:T(8,128)}) custom-call(bf16[256,128]{1,0:T(8,128)(2,1)} %sig_ref.1, s32[8,256]{1,0:T(8,128)} %broadcast_in_dim.11.idx_ref, bf16[256,512]{1,0:T(8,128)(2,1)} %latents_ref.1, bf16[32,512]{1,0:T(8,128)(2,1)} %w_in_ref.1, bf16[512,512]{1,0:T(8,128)(2,1)} %w_query_ref.1, f32[2,512]{1,0:T(2,128)} %bias_ref.1, ...), custom_call_target="tpu_custom_call" | custom-call | tf_op jit(solution)/shard_map/pallas_call | solution.py:688
  66.9 1.6 %copy.17 = bf16[4,32,512]{2,1,0:T(8,128)(2,1)} copy(bf16[4,32,512]{2,1,0:T(8,128)(2,1)} %get-tuple-element.4) | data formatting | bytes 262144
  68.5 1.9 %copy.18 = f32[256,512]{1,0:T(8,128)} copy(f32[256,512]{1,0:T(8,128)} %get-tuple-element.5) | data formatting | bytes 1048576
